TPU v7x, 256 devices: a whole 4x4x8 slice. The times are simulated.
256 devices in a mesh: sect: 2 (over y_hi), gx: 16 (over x, y_lo, core), yz: 8 (over z).
Axes of the slice: x: 4, y: 4 (y_hi: 2, y_lo: 2; y = y_hi * 2 + y_lo), z: 8, core: 2. Of those that a mesh axis runs over, the one named last changes fastest.
Arguments:
- fields: float32 [2, 5, 128, 32768], P('sect', None, 'gx', 'yz'), may hold values from -6 to 6
- jacobians: float32 [3, 5, 5], replicated, may hold values from -2.5 to 2.5
- inflow_map: int32 [128], P('yz'), may hold values from 0 to 127
- donor_tiles: int32 [2, 16, 8, 64, 3], P('sect', 'gx', 'yz'), may hold values from 0 to 247, as said below
- receptor_tiles: int32 [2, 16, 8, 64], P('sect', 'gx', 'yz'), may hold values from 0 to 64, as said below
Outputs:
- segment_fields: float32 [2, 5, 128, 32768], P('sect', None, 'gx', 'yz')
Inputs may be any that keep to these rules, and one draw needn't show every extreme that they name: `donor_tiles`: each row holds a tile index along x below 1, a tile index along y below 2, and a first z cell. `receptor_tiles`: entry s * 4 + m names the tile of the receiving block that takes slot m from block s along gx; 64 marks an empty slot. In every group along gx some block has all slots live.
All inputs are finite; a program needn't handle non-finite values.
Results may differ from a plain program's by a relative error of at most 0.0003.
Values sent between devices are 32-bit elements; how exact they have to be, the bound alone decides.
A program may use at most 128 MiB of HBM per device.

v0:
```python
import functools

import jax
import jax.numpy as jnp
import ml_dtypes
import numpy as np
from jax import lax
from jax.experimental import pallas as pl
from jax.experimental.pallas import tpu as pltpu
from jax.sharding import PartitionSpec as P

MESH = pl.DeviceIdType.MESH
F32 = jnp.float32
BF16 = jnp.bfloat16

CX = 8
CY = 16
CZ = 256
NG = 16
NK = 8
NX = 128
NY = 128
SLOTS = 64

SEGMENT_STEP = 0.25
SIDE_DERIV = 1.0 / 3.0
SIDE_FILTER = 0.49


def filter_coeffs():
    side = SIDE_FILTER
    return [
        (193 + 126 * side) / 256,
        (105 + 302 * side) / 256,
        15 * (-1 + 2 * side) / 64,
        45 * (1 - 2 * side) / 512,
        5 * (-1 + 2 * side) / 256,
        (1 - 2 * side) / 512,
    ]


DERIV_STENCIL = ((1, 7.0 / 9.0), (-1, -7.0 / 9.0), (2, 1.0 / 36.0), (-2, -1.0 / 36.0))
FILTER_STENCIL = ((0, filter_coeffs()[0]),) + tuple(
    (sign * reach, filter_coeffs()[reach] / 2) for reach in range(1, 6) for sign in (1, -1)
)


def sides(length, periodic, stencil, side):
    left = np.eye(length)
    right = np.zeros((length, length))
    for row in range(length):
        for offset, factor in ((-1, side), (1, side)):
            if periodic or 0 <= row + offset < length:
                left[row, (row + offset) % length] += factor
        for offset, factor in stencil:
            if periodic or 0 <= row + offset < length:
                right[row, (row + offset) % length] += factor
    return left, right


def line_matrix(length, periodic, stencil, side):
    return np.linalg.solve(*sides(length, periodic, stencil, side))


def halves(matrix):
    value = np.asarray(matrix, np.float32)
    high = value.astype(ml_dtypes.bfloat16)
    low = (value - high.astype(np.float32)).astype(ml_dtypes.bfloat16)
    return np.stack([high, low])


def block_table(stencil, side):
    left, right = sides(NY, False, stencil, side)
    reach = max(offset for offset, _ in stencil)
    below = np.zeros((NK, NY))
    above = np.zeros((NK, NY))
    corner_low = np.zeros(NK)
    corner_high = np.zeros(NK)
    for d in range(NK):
        lo, hi = d * CY, (d + 1) * CY
        if d > 0:
            row = np.linalg.solve(left[:lo, :lo].T, np.eye(lo)[lo - 1])
            below[d] = -side * (row @ right[:lo])
            corner_low[d] = row[-1]
        if d < NK - 1:
            row = np.linalg.solve(left[hi:, hi:].T, np.eye(NY - hi)[0])
            above[d] = -side * (row @ right[hi:])
            corner_high[d] = row[0]
    send_up = np.zeros((NK, CY))
    send_down = np.zeros((NK, CY))
    for s in range(NK):
        cells = slice(s * CY, (s + 1) * CY)
        if s < NK - 1:
            value = below[min(s + 2, NK - 1)][cells]
            send_up[s] = value / np.abs(value).max()
        if s > 0:
            value = above[max(s - 2, 0)][cells]
            send_down[s] = value / np.abs(value).max()
    take_low = np.zeros((NK, NK))
    take_high = np.zeros((NK, NK))
    near_low = np.zeros((NK, reach))
    near_high = np.zeros((NK, reach))
    own_low = np.zeros((NK, reach))
    own_high = np.zeros((NK, reach))
    for d in range(NK):
        for s in range(d):
            value, unit = below[d][s * CY : (s + 1) * CY], send_up[s]
            core = unit[: CY - reach]
            take_low[d, s] = (value[: CY - reach] @ core) / (core @ core)
            if s == d - 1:
                near_low[d] = (value - take_low[d, s] * unit)[CY - reach :]
        for s in range(d + 1, NK):
            value, unit = above[d][s * CY : (s + 1) * CY], send_down[s]
            core = unit[reach:]
            take_high[d, s] = (value[reach:] @ core) / (core @ core)
            if s == d + 1:
                near_high[d] = (value - take_high[d, s] * unit)[:reach]
        own_low[d] = below[d][d * CY : d * CY + reach]
        own_high[d] = above[d][(d + 1) * CY - reach : (d + 1) * CY]
    lower = np.zeros((NK, CY))
    inverse = np.zeros((NK, CY))
    for d in range(NK):
        diagonal = np.ones(CY)
        diagonal[0] -= side**2 * corner_low[d]
        diagonal[-1] -= side**2 * corner_high[d]
        inverse[d, 0] = 1 / diagonal[0]
        for y in range(1, CY):
            lower[d, y] = side * inverse[d, y - 1]
            inverse[d, y] = 1 / (diagonal[y] - side * lower[d, y])
    has_low = (np.arange(NK) > 0).astype(np.float64)[:, None]
    has_high = (np.arange(NK) < NK - 1).astype(np.float64)[:, None]
    parts = dict(
        send_up=send_up, send_down=send_down, take_low=take_low, take_high=take_high, near_low=near_low,
        near_high=near_high, own_low=own_low, own_high=own_high, lower=lower, inverse=inverse,
        has_low=has_low, has_high=has_high,
    )
    places, start = {}, 0
    for name, value in parts.items():
        places[name] = start
        start += value.shape[1]
    return np.concatenate(list(parts.values()), axis=1), places, reach


def split(value):
    high = value.astype(BF16)
    low = (value - high.astype(F32)).astype(BF16)
    return high, low


def dot(a, b, dims=((1,), (0,))):
    return lax.dot_general(a, b, (dims, ((), ())), preferred_element_type=F32)


def kernel(
    places_d, places_f, width,
    fields, jac, inflow, donors, receptors, table, dx, fx, dz, fz, out,
    u0, sel, place, ts, tr, u, pu, dy, q, pq, gx_, gz_, pp, ps, sb,
    outlet, inlet, phi_s, phi_d, phi_t, phi_f, low_d, high_d, low_f, high_f,
    tile_s, tile_r, u_s, u_r, q_s, q_r, s_s, s_r, pd_s, pd_r, pf_s, pf_r, h_s, h_r, in_s, in_r,
):
    sect = lax.axis_index("sect")
    g = lax.axis_index("gx")
    k = lax.axis_index("yz")
    here = k * width

    def along_gx(j):
        return lax.rem(g + j, NG)

    def from_gx(j):
        return lax.rem(g + NG - j, NG)

    def along_yz(j):
        return lax.rem(k + j, NK)

    def from_yz(j):
        return lax.rem(k + NK - j, NK)

    is_outlet = jnp.logical_and(sect == 0, g == 0)
    is_inlet = jnp.logical_and(sect == 1, g == 0)

    barrier = pltpu.get_barrier_semaphore()

    @pl.loop(1, NG)
    def _(j):
        pl.semaphore_signal(barrier, inc=1, device_id={"gx": along_gx(j)}, device_id_type=MESH)

    @pl.loop(1, NK)
    def _(j):
        pl.semaphore_signal(barrier, inc=1, device_id={"yz": along_yz(j)}, device_id_type=MESH)

    @pl.when(is_inlet)
    def _():
        @pl.loop(0, NK)
        def _(j):
            pl.semaphore_signal(barrier, inc=1, device_id={"sect": 0, "yz": j}, device_id_type=MESH)

    @pl.when(is_outlet)
    def _():
        for y in range(CY):
            for f in range(5):
                outlet[y : y + 1, f * CZ : (f + 1) * CZ] = fields[0, f, CX - 1 : CX, y * CZ : (y + 1) * CZ]

    @pl.when(jnp.logical_not(is_outlet))
    def _():
        pl.semaphore_wait(barrier, NG + NK - 2)

    @pl.when(is_outlet)
    def _():
        pl.semaphore_wait(barrier, NG + 2 * NK - 2)

        @pl.loop(0, NK)
        def _(j):
            pltpu.make_async_remote_copy(
                outlet, inlet.at[pl.ds(k * CY, CY)], in_s.at[j], in_r.at[k],
                device_id={"sect": 1, "yz": j}, device_id_type=MESH,
            ).start()

    for y in range(CY):
        for f in range(5):
            u0[y, f] = fields[0, f, :, y * CZ : (y + 1) * CZ]

    offset = lax.broadcasted_iota(jnp.int32, (8, CZ), 1) - lax.broadcasted_iota(jnp.int32, (8, CZ), 0)

    @pl.loop(0, SLOTS // 2)
    def _(j):
        for b in range(2):
            rows = []
            for e in range(2):
                slot = 2 * j + e
                first = jnp.where(donors[slot * 3 + 1] == b, donors[slot * 3 + 2], -1000)
                hit = jnp.logical_or(offset == first, offset == first + 1)
                rows.append(jnp.where(hit, 0.5, 0.0))
            sel[b, pl.ds(pl.multiple_of(16 * j, 16), 16), :] = jnp.concatenate(rows, axis=0).astype(BF16)

    ts[:, :, 256:384] = jnp.zeros((NG, 32, 128), F32)

    @pl.when(is_inlet)
    def _():
        @pl.loop(0, NK)
        def _(j):
            pltpu.make_async_remote_copy(
                outlet, inlet.at[pl.ds(j * CY, CY)], in_s.at[j], in_r.at[j],
                device_id={"sect": 1, "yz": j}, device_id_type=MESH,
            ).wait_recv()

        for y in range(CY):
            row = inlet[pl.ds(inflow[y], 1), :]
            for f in range(5):
                u0[y, f, 0:1, :] = row[:, f * CZ : (f + 1) * CZ]

    payload = None
    for b in range(2):
        for part in split(u0[8 * b : 8 * b + 8].reshape(320, CZ)):
            term = dot(sel[b], part, ((1,), (1,)))
            payload = term if payload is None else payload + term
    ts[:, :, 0:320] = payload.reshape(NG, 32, 320)

    def all_to_all(source, target, send, receive, j):
        return pltpu.make_async_remote_copy(
            source.at[along_gx(j)], target.at[g], send.at[j], receive.at[j],
            device_id={"gx": along_gx(j)}, device_id_type=MESH,
        )

    def arrive_all(source, target, send, receive):
        @pl.loop(1, NG)
        def _(j):
            pltpu.make_async_remote_copy(
                source.at[along_gx(j)], target.at[from_gx(j)], send.at[j], receive.at[j],
                device_id={"gx": along_gx(j)}, device_id_type=MESH,
            ).wait_recv()

    @pl.loop(1, NG)
    def _(j):
        all_to_all(ts, tr, tile_s, tile_r, j).start()

    tr[g] = ts[g]

    def place_row(j, counts):
        counts = list(counts)
        for t in range(2):
            rows = []
            for e in range(2):
                goal = (receptors[2 * j + e] - 32 * t) * 8
                one = jnp.where(offset == goal, 1.0, 0.0)
                counts[t] = counts[t] + one
                rows.append(one)
            place[t, pl.ds(pl.multiple_of(16 * j, 16), 16), :] = jnp.concatenate(rows, axis=0).astype(BF16)
        return tuple(counts)

    counts = lax.fori_loop(0, SLOTS // 2, place_row, (jnp.zeros((8, CZ), F32),) * 2)

    arrive_all(ts, tr, tile_s, tile_r)

    received = split(tr[...].reshape(512, 384))
    for t in range(2):
        total = dot(received[0], place[t], ((0,), (0,))) + dot(received[1], place[t], ((0,), (0,)))
        hits = jnp.sum(counts[t], axis=0, keepdims=True)
        scale = (1.0 / jnp.maximum(hits, 1.0)).reshape(1, 1, 1, CZ)
        mean = total[:320].reshape(8, 5, 8, CZ) * scale
        u[8 * t : 8 * t + 8] = jnp.where(hits.reshape(1, 1, 1, CZ) > 0, mean, u0[8 * t : 8 * t + 8])

    @pl.loop(1, NG)
    def _(j):
        all_to_all(u, pu, u_s, u_r, j).start()

    pu[g] = u[g]

    def neighbours(source, low, high, reach, base):
        up = pltpu.make_async_remote_copy(
            source.at[pl.ds(CY - reach, reach)], low, h_s.at[base], h_r.at[base],
            device_id={"yz": along_yz(1)}, device_id_type=MESH,
        )
        down = pltpu.make_async_remote_copy(
            source.at[pl.ds(0, reach)], high, h_s.at[base + 1], h_r.at[base + 1],
            device_id={"yz": from_yz(1)}, device_id_type=MESH,
        )
        return up, down

    def spread(planes, target, send, receive, j):
        peer = along_yz(j)
        which = lax.div(k - peer + NK, NK)
        return pltpu.make_async_remote_copy(
            planes.at[which], target.at[k], send.at[j], receive.at[j], device_id={"yz": peer}, device_id_type=MESH,
        )

    def make_planes(source, planes, places):
        @pl.loop(0, 5)
        def _(f):
            up = down = None
            for y in range(CY):
                row = source[y, f]
                a = table[here + places["send_up"] + y] * row
                b = table[here + places["send_down"] + y] * row
                up, down = (a, b) if up is None else (up + a, down + b)
            planes[0, f] = up
            planes[1, f] = down

    def spread_out(source, planes, target, send, receive, low, high, reach, base):
        for copy in neighbours(source, low, high, reach, base):
            copy.start()

        @pl.loop(1, NK)
        def _(j):
            spread(planes, target, send, receive, j).start()

    def spread_in(source, planes, target, send, receive, low, high, reach, base):
        for copy in neighbours(source, low, high, reach, base):
            copy.wait_recv()

        @pl.loop(1, NK)
        def _(j):
            pltpu.make_async_remote_copy(
                planes.at[0], target.at[from_yz(j)], send.at[j], receive.at[j],
                device_id={"yz": along_yz(j)}, device_id_type=MESH,
            ).wait_recv()

    def y_lines(source, gathered, low, high, places, reach, stencil, side, store):
        def entry(name, index=0):
            return table[here + places[name] + index]

        @pl.loop(0, 5)
        def _(f):
            for half in range(2):
                lanes = slice(128 * half, 128 * half + 128)
                from_low = from_high = None
                for j in range(1, NK):
                    s = from_yz(j)
                    plane = gathered[s, f, :, lanes]
                    a = table[here + places["take_low"] + s] * plane
                    b = table[here + places["take_high"] + s] * plane
                    from_low, from_high = (a, b) if from_low is None else (from_low + a, from_high + b)
                rows = [low[h, f, :, lanes] * entry("has_low") for h in range(reach)]
                rows += [source[y, f, :, lanes] for y in range(CY)]
                rows += [high[h, f, :, lanes] * entry("has_high") for h in range(reach)]
                for h in range(reach):
                    from_low += entry("near_low", h) * rows[h] + entry("own_low", h) * rows[reach + h]
                    from_high += entry("near_high", h) * rows[reach + CY + h] + entry("own_high", h) * rows[CY + h]
                pairs = {}
                for move, factor in stencil:
                    pairs.setdefault(abs(move), {})[move] = factor
                values = []
                for y in range(CY):
                    at = reach + y
                    value = None
                    for move, factors in pairs.items():
                        if move == 0:
                            term = np.float32(factors[0]) * rows[at]
                        elif factors[move] == factors[-move]:
                            term = np.float32(factors[move]) * (rows[at + move] + rows[at - move])
                        else:
                            term = np.float32(factors[move]) * (rows[at + move] - rows[at - move])
                        value = term if value is None else value + term
                    if y == 0:
                        value = value + from_low
                    if y == CY - 1:
                        value = value + from_high
                    if y > 0:
                        value = value - entry("lower", y) * values[-1]
                    values.append(value)
                last = None
                for y in range(CY - 1, -1, -1):
                    value = values[y] if last is None else values[y] - np.float32(side) * last
                    last = value * entry("inverse", y)
                    store(y, f, half, last)

    deriv = (u, phi_s, phi_d, pd_s, pd_r, low_d, high_d, 2, 0)
    make_planes(u, phi_s, places_d)
    spread_out(*deriv)
    spread_in(*deriv)

    def store_dy(y, f, half, value):
        dy[y, f, :, 128 * half : 128 * half + 128] = value

    y_lines(u, phi_d, low_d, high_d, places_d, 2, DERIV_STENCIL, SIDE_DERIV, store_dy)

    def mix(d, f, h):
        return jac[d * 25 + f * 5 + h] * (-SEGMENT_STEP)

    @pl.loop(1, NG + 1)
    def _(j):
        y = along_gx(j)
        slopes = [dy[y, h] for h in range(5)]
        for f in range(5):
            value = mix(1, f, 0) * slopes[0]
            for h in range(1, 5):
                value += mix(1, f, h) * slopes[h]
            q[y, f] = value

        @pl.when(j < NG)
        def _():
            all_to_all(q, pq, q_s, q_r, j).start()

    pq[g] = q[g]

    arrive_all(u, pu, u_s, u_r)
    for f in range(5):
        lines = pu[:, f].reshape(NX, CZ)
        high, low = split(lines)
        gx_[f] = dot(dx[sect, 0], high) + dot(dx[sect, 0], low) + dot(dx[sect, 1], high)
        gz_[f] = dot(high, dz[0]) + dot(low, dz[0]) + dot(high, dz[1])

    @pl.loop(0, 5)
    def _(f):
        value = pu[:, f].reshape(NX, CZ)
        for h in range(5):
            value += jac[f * 5 + h] * (-SEGMENT_STEP) * gx_[h]
            value += jac[50 + f * 5 + h] * (-SEGMENT_STEP) * gz_[h]
        pp[f] = value

    arrive_all(q, pq, q_s, q_r)
    for f in range(5):
        high, low = split(pp[f] + pq[:, f].reshape(NX, CZ))
        smooth = dot(high, fz[0]) + dot(low, fz[0]) + dot(high, fz[1])
        high, low = split(smooth)
        smooth = dot(fx[sect, 0], high) + dot(fx[sect, 0], low) + dot(fx[sect, 1], high)
        ps[:, f] = smooth.reshape(NG, CX, CZ)

    @pl.loop(1, NG)
    def _(j):
        all_to_all(ps, sb, s_s, s_r, j).start()

    sb[g] = ps[g]
    arrive_all(ps, sb, s_s, s_r)

    smooth = (sb, phi_t, phi_f, pf_s, pf_r, low_f, high_f, 5, 2)
    make_planes(sb, phi_t, places_f)
    spread_out(*smooth)
    spread_in(*smooth)

    def store_out(y, f, half, value):
        start = y * CZ + 128 * half
        out[0, f, :, start : start + 128] = value

    y_lines(sb, phi_f, low_f, high_f, places_f, 5, FILTER_STENCIL, SIDE_FILTER, store_out)

    @pl.loop(1, NG)
    def _(j):
        all_to_all(ts, tr, tile_s, tile_r, j).wait_send()
        all_to_all(u, pu, u_s, u_r, j).wait_send()
        all_to_all(q, pq, q_s, q_r, j).wait_send()
        all_to_all(ps, sb, s_s, s_r, j).wait_send()

    @pl.loop(1, NK)
    def _(j):
        spread(phi_s, phi_d, pd_s, pd_r, j).wait_send()
        spread(phi_t, phi_f, pf_s, pf_r, j).wait_send()

    for copy in neighbours(u, low_d, high_d, 2, 0) + neighbours(sb, low_f, high_f, 5, 2):
        copy.wait_send()

    @pl.when(is_outlet)
    def _():
        @pl.loop(0, NK)
        def _(j):
            pltpu.make_async_remote_copy(
                outlet, inlet.at[pl.ds(k * CY, CY)], in_s.at[j], in_r.at[k],
                device_id={"sect": 1, "yz": j}, device_id_type=MESH,
            ).wait_send()


def per_device(fields, jacobians, inflow_map, donor_tiles, receptor_tiles):
    table_d, places_d, reach_d = block_table(DERIV_STENCIL, SIDE_DERIV)
    table_f, places_f, reach_f = block_table(FILTER_STENCIL, SIDE_FILTER)
    places_f = {name: start + table_d.shape[1] for name, start in places_f.items()}
    table = np.concatenate([table_d, table_f], axis=1).astype(np.float32)
    width = table.shape[1]
    dx = np.stack([halves(line_matrix(NX, p, DERIV_STENCIL, SIDE_DERIV)) for p in (True, False)])
    fx = np.stack([halves(line_matrix(NX, p, FILTER_STENCIL, SIDE_FILTER)) for p in (True, False)])
    dz = halves(line_matrix(CZ, True, DERIV_STENCIL, SIDE_DERIV).T)
    fz = halves(line_matrix(CZ, True, FILTER_STENCIL, SIDE_FILTER).T)
    vmem = pl.BlockSpec(memory_space=pltpu.VMEM)
    smem = pl.BlockSpec(memory_space=pltpu.SMEM)
    block = (CY, 5, CX, CZ)
    planes = (5, CX, CZ)

    def buffer(*shape, kind=F32):
        return pltpu.VMEM(shape, kind)

    dma = pltpu.SemaphoreType.DMA
    return pl.pallas_call(
        functools.partial(kernel, places_d, places_f, width),
        out_shape=jax.ShapeDtypeStruct(fields.shape, F32),
        in_specs=[vmem, smem, smem, smem, smem, smem, vmem, vmem, vmem, vmem],
        out_specs=vmem,
        scratch_shapes=[
            buffer(*block),
            buffer(2, 512, CZ, kind=BF16), buffer(2, 512, CZ, kind=BF16),
            buffer(NG, 32, 384), buffer(NG, 32, 384),
            buffer(*block), buffer(*block), buffer(*block), buffer(*block), buffer(*block),
            buffer(5, NX, CZ), buffer(5, NX, CZ), buffer(5, NX, CZ),
            buffer(*block), buffer(*block),
            buffer(CY, 5 * CZ), buffer(NY, 5 * CZ),
            buffer(2, *planes), buffer(NK, *planes), buffer(2, *planes), buffer(NK, *planes),
            buffer(2, *planes), buffer(2, *planes), buffer(5, *planes), buffer(5, *planes),
            dma((NG,)), dma((NG,)), dma((NG,)), dma((NG,)), dma((NG,)), dma((NG,)), dma((NG,)), dma((NG,)),
            dma((NK,)), dma((NK,)), dma((NK,)), dma((NK,)), dma((4,)), dma((4,)), dma((NK,)), dma((NK,)),
        ],
        compiler_params=pltpu.CompilerParams(
            collective_id=0, has_side_effects=True, vmem_limit_bytes=48 * 1024 * 1024
        ),
        name="segment",
    )(
        fields, jacobians.reshape(75), inflow_map, donor_tiles.reshape(3 * SLOTS), receptor_tiles.reshape(SLOTS),
        jnp.asarray(table.reshape(-1)), jnp.asarray(dx), jnp.asarray(fx), jnp.asarray(dz), jnp.asarray(fz),
    )


def solution(mesh):
    in_specs = (
        P("sect", None, "gx", "yz"),
        P(),
        P("yz"),
        P("sect", "gx", "yz", None, None),
        P("sect", "gx", "yz", None),
    )
    out_specs = P("sect", None, "gx", "yz")
    return jax.shard_map(
        per_device, mesh=mesh, in_specs=in_specs, out_specs=out_specs, check_vma=False
    )
```

profile of v0, /device:TPU:28, one launch (start us, length us, event | category | flops | bytes accessed | tf_op | source)
XLA Modules:
  0.0 100.5 jit_solution(9048946397886776412)
XLA Ops:
  0.0 0.7 copy.12
  0.7 0.0 copy-start.8
  0.7 0.1 reshape.9.jac
  0.8 0.6 copy-done.8
  1.4 0.1 copy.13
  1.5 0.0 copy-start.5
  1.5 0.0 copy-start.6
  1.5 0.0 copy-start.7
  1.5 0.1 reshape.10.donors
  1.6 0.5 copy-done.5
  2.2 0.0 copy-done.6
  2.2 0.0 copy-done.7
  2.2 0.0 copy-start
  2.2 1.1 %copy-done = f32[1,5,8,4096]{3,2,1,0:T(8,128)S(1)} copy-done((f32[1,5,8,4096]{3,2,1,0:T(8,128)S(1)}, f32[1,5,8,4096]{3,2,1,0:T(8,128)}, u32[]{:S(2)}) %copy-start) | copy-done | bytes 655384
  3.3 0.0 copy-start.1
  3.3 0.9 copy-done.1
  4.2 0.0 copy-start.2
  4.2 0.9 copy-done.2
  5.2 0.0 copy-start.3
  5.2 0.9 copy-done.3
  6.1 0.0 copy-start.4
  6.1 0.9 copy-done.4
  7.0 92.7 %segment.1 = f32[1,5,8,4096]{3,2,1,0:T(8,128)S(1)} custom-call(f32[1,5,8,4096]{3,2,1,0:T(8,128)S(1)} %copy-done, f32[75]{0:T(128)S(1)} %reshape.9.jac, s32[16]{0:T(128)S(1)} %copy-done.6, s32[192]{0:T(256)S(1)} %reshape.10.donors, s32[64]{0:T(128)S(1)} %bitcast.3, f32[1536]{0:T(1024)S(1)} %copy-done.5, bf16[2,2,128,128]{3,2,1,0:T(8,128)(2,1)S(1)} %copy-done.4, ...), custom_call_target="tpu_custom_call" | custom-call | tf_op jit(solution)/shard_map/segment/pallas_call | solution.py:520
  99.7 0.8 copy.15
Async XLA Ops:
  0.7 0.7 copy-start.8
  1.5 0.7 copy-start.5
  1.5 0.7 copy-start.6
  1.5 0.7 copy-start.7
  2.2 1.1 %copy-start = (f32[1,5,8,4096]{3,2,1,0:T(8,128)S(1)}, f32[1,5,8,4096]{3,2,1,0:T(8,128)}, u32[]{:S(2)}) copy-start(f32[1,5,8,4096]{3,2,1,0:T(8,128)} %fields.1) | copy-start | bytes 1966084
  3.3 0.9 copy-start.1
  4.2 0.9 copy-start.2
  5.2 0.9 copy-start.3
  6.1 0.9 copy-start.4
where the time goes:
time: 101 us
  Pallas kernels  92.7 us (92%)
  local copies, waits for them, and re-layouts  7.79 us (8%)
    pallas_call x1, Pallas kernels, per_device(): pl.pallas_call(functools.partial(kernel, places_d, places_f, width), out_...  92.7 us
    unnamed x21, local copies, waits for them, and re-layouts  7.58 us

commit v1 on v0

v1 whole, which is shorter than its diff:
```python
import functools

import jax
import jax.numpy as jnp
import ml_dtypes
import numpy as np
from jax import lax
from jax.experimental import pallas as pl
from jax.experimental.pallas import tpu as pltpu
from jax.sharding import PartitionSpec as P

MESH = pl.DeviceIdType.MESH
HBM = pltpu.MemorySpace.HBM
F32 = jnp.float32
BF16 = jnp.bfloat16

CX = 8
CY = 16
CZ = 256
NG = 16
NK = 8
NX = 128
NY = 128
SLOTS = 64
GROUPS = ((0, 2), (2, 4), (4, 5))
VMEM_MIB = 62
INLET_ORDER = (4, 3, 5, 2, 6, 1, 7)
DIRECT_DERIV = 0
DIRECT_FILTER = 2

SEGMENT_STEP = 0.25
SIDE_DERIV = 1.0 / 3.0
SIDE_FILTER = 0.49


def filter_coeffs():
    side = SIDE_FILTER
    return [
        (193 + 126 * side) / 256,
        (105 + 302 * side) / 256,
        15 * (-1 + 2 * side) / 64,
        45 * (1 - 2 * side) / 512,
        5 * (-1 + 2 * side) / 256,
        (1 - 2 * side) / 512,
    ]


DERIV_STENCIL = ((1, 7.0 / 9.0), (-1, -7.0 / 9.0), (2, 1.0 / 36.0), (-2, -1.0 / 36.0))
FILTER_STENCIL = ((0, filter_coeffs()[0]),) + tuple(
    (sign * reach, filter_coeffs()[reach] / 2) for reach in range(1, 6) for sign in (1, -1)
)


def sides(length, periodic, stencil, side):
    left = np.eye(length)
    right = np.zeros((length, length))
    for row in range(length):
        for offset, factor in ((-1, side), (1, side)):
            if periodic or 0 <= row + offset < length:
                left[row, (row + offset) % length] += factor
        for offset, factor in stencil:
            if periodic or 0 <= row + offset < length:
                right[row, (row + offset) % length] += factor
    return left, right


def line_matrix(length, periodic, stencil, side):
    return np.linalg.solve(*sides(length, periodic, stencil, side))


def halves(matrix):
    value = np.asarray(matrix, np.float32)
    high = value.astype(ml_dtypes.bfloat16)
    low = (value - high.astype(np.float32)).astype(ml_dtypes.bfloat16)
    return np.stack([high, low])


def block_table(stencil, side):
    left, right = sides(NY, False, stencil, side)
    reach = max(offset for offset, _ in stencil)
    below = np.zeros((NK, NY))
    above = np.zeros((NK, NY))
    corner_low = np.zeros(NK)
    corner_high = np.zeros(NK)
    for d in range(NK):
        lo, hi = d * CY, (d + 1) * CY
        if d > 0:
            row = np.linalg.solve(left[:lo, :lo].T, np.eye(lo)[lo - 1])
            below[d] = -side * (row @ right[:lo])
            corner_low[d] = row[-1]
        if d < NK - 1:
            row = np.linalg.solve(left[hi:, hi:].T, np.eye(NY - hi)[0])
            above[d] = -side * (row @ right[hi:])
            corner_high[d] = row[0]
    send_up = np.zeros((NK, CY))
    send_down = np.zeros((NK, CY))
    for s in range(NK):
        cells = slice(s * CY, (s + 1) * CY)
        if s < NK - 1:
            value = below[min(s + 2, NK - 1)][cells]
            send_up[s] = value / np.abs(value).max()
        if s > 0:
            value = above[max(s - 2, 0)][cells]
            send_down[s] = value / np.abs(value).max()
    take_low = np.zeros((NK, NK))
    take_high = np.zeros((NK, NK))
    near_low = np.zeros((NK, reach))
    near_high = np.zeros((NK, reach))
    own_low = np.zeros((NK, reach))
    own_high = np.zeros((NK, reach))
    for d in range(NK):
        for s in range(d):
            value, unit = below[d][s * CY : (s + 1) * CY], send_up[s]
            core = unit[: CY - reach]
            take_low[d, s] = (value[: CY - reach] @ core) / (core @ core)
            if s == d - 1:
                near_low[d] = (value - take_low[d, s] * unit)[CY - reach :]
        for s in range(d + 1, NK):
            value, unit = above[d][s * CY : (s + 1) * CY], send_down[s]
            core = unit[reach:]
            take_high[d, s] = (value[reach:] @ core) / (core @ core)
            if s == d + 1:
                near_high[d] = (value - take_high[d, s] * unit)[:reach]
        own_low[d] = below[d][d * CY : d * CY + reach]
        own_high[d] = above[d][(d + 1) * CY - reach : (d + 1) * CY]
    lower = np.zeros((NK, CY))
    inverse = np.zeros((NK, CY))
    for d in range(NK):
        diagonal = np.ones(CY)
        diagonal[0] -= side**2 * corner_low[d]
        diagonal[-1] -= side**2 * corner_high[d]
        inverse[d, 0] = 1 / diagonal[0]
        for y in range(1, CY):
            lower[d, y] = side * inverse[d, y - 1]
            inverse[d, y] = 1 / (diagonal[y] - side * lower[d, y])
    has_low = (np.arange(NK) > 0).astype(np.float64)
    has_high = (np.arange(NK) < NK - 1).astype(np.float64)
    parts = dict(
        send_up=send_up, send_down=send_down, take=np.stack([take_low, take_high]), near_low=near_low,
        near_high=near_high, own_low=own_low, own_high=own_high, lower=lower, inverse=inverse,
        has_low=has_low, has_high=has_high,
    )
    places, start = {}, 0
    for name, value in parts.items():
        places[name] = start
        start += value.size
    return np.concatenate([value.reshape(-1) for value in parts.values()]), places


def split(value):
    high = value.astype(BF16)
    low = (value - high.astype(F32)).astype(BF16)
    return high, low


def dot(a, b, dims=((1,), (0,))):
    return lax.dot_general(a, b, (dims, ((), ())), preferred_element_type=F32)


def kernel(
    at_d, at_f,
    fields_hbm, jac_hbm, inflow_hbm, donors_hbm, receptors_hbm, table_hbm, dx_hbm, fx_hbm, dz_hbm, fz_hbm, out,
    fields, jac, inflow, donors, receptors, table, dx, fx, dz, fz, load_sem,
    u0, sel, place, ts, tr, u, pu, v, q, pq, gx_, gz_, pp, ps, sb,
    outlet, inlet, inlet_rows, patch_s, patch_r,
    phi_d, col_d, gam_d, got_d, phi_f, col_f, gam_f, got_f, edge_d, edge_f, planes_d, everyone_d, planes_f, everyone_f,
    tile_ss, tile_rs, u_ss, u_rs, q_ss, q_rs, s_ss, s_rs,
    d1_ss, d1_rs, d2_ss, d2_rs, f1_ss, f1_rs, f2_ss, f2_rs, dh_ss, dh_rs, fh_ss, fh_rs, in_ss, in_rs, patch_ss, patch_rs,
):
    sect = lax.axis_index("sect")
    g = lax.axis_index("gx")
    k = lax.axis_index("yz")

    def along_gx(j):
        return lax.rem(g + j, NG)

    def along_yz(j):
        return lax.rem(k + j, NK)

    def from_yz(j):
        return lax.rem(k + NK - j, NK)

    is_outlet = jnp.logical_and(sect == 0, g == 0)
    is_inlet = jnp.logical_and(sect == 1, g == 0)

    barrier = pltpu.get_barrier_semaphore()

    @pl.loop(1, NG)
    def _(j):
        pl.semaphore_signal(barrier, inc=1, device_id={"gx": along_gx(j)}, device_id_type=MESH)

    @pl.loop(1, NK)
    def _(j):
        pl.semaphore_signal(barrier, inc=1, device_id={"yz": along_yz(j)}, device_id_type=MESH)

    @pl.when(is_inlet)
    def _():
        pl.semaphore_signal(barrier, inc=1, device_id={"sect": 0}, device_id_type=MESH)

    pairs = (
        (fields_hbm, fields), (donors_hbm, donors), (receptors_hbm, receptors), (inflow_hbm, inflow),
        (jac_hbm, jac), (table_hbm, table), (dx_hbm, dx), (dz_hbm, dz), (fz_hbm, fz), (fx_hbm, fx),
    )
    loads = [pltpu.make_async_copy(source, target, load_sem.at[i]) for i, (source, target) in enumerate(pairs)]
    for load in loads:
        load.start()
    loads[0].wait()

    mine = pl.ds(pl.multiple_of(k * CY, CY), CY)

    def inflow_copy():
        return pltpu.make_async_remote_copy(
            outlet, inlet.at[mine], in_ss.at[0], in_rs.at[0], device_id={"sect": 1}, device_id_type=MESH,
        )

    def inlet_copies():
        whole = inlet.at[0 : NY - CY]
        return pltpu.make_async_remote_copy(
            whole, whole, in_ss.at[1], in_rs.at[1], device_id={"yz": along_yz(1)}, device_id_type=MESH,
        )

    @pl.when(is_outlet)
    def _():
        for y in range(CY):
            for f in range(5):
                outlet[y : y + 1, f * CZ : (f + 1) * CZ] = fields[0, f, CX - 1 : CX, y * CZ : (y + 1) * CZ]

        pl.semaphore_wait(barrier, NG + NK - 1)
        inflow_copy().start()

    for y in range(CY):
        for f in range(5):
            u0[y, f] = fields[0, f, :, y * CZ : (y + 1) * CZ]

    @pl.when(is_inlet)
    def _():
        for y in range(CY):
            for f in range(5):
                u0[y, f, 0:1, :] = jnp.zeros((1, CZ), F32)

    offset = lax.broadcasted_iota(jnp.int32, (8, CZ), 1) - lax.broadcasted_iota(jnp.int32, (8, CZ), 0)
    loads[1].wait()

    @pl.loop(0, SLOTS // 2)
    def _(j):
        for b in range(2):
            rows = []
            for e in range(2):
                slot = 2 * j + e
                first = jnp.where(donors[0, 0, 1, 0, slot] == b, donors[0, 0, 2, 0, slot], -1000)
                hit = jnp.logical_or(offset == first, offset == first + 1)
                rows.append(jnp.where(hit, 0.5, 0.0))
            sel[b, pl.ds(pl.multiple_of(16 * j, 16), 16), :] = jnp.concatenate(rows, axis=0).astype(BF16)

    payload = None
    for b in range(2):
        lines = jnp.concatenate([u0[8 * b : 8 * b + 8].reshape(320, CZ), jnp.zeros((64, CZ), F32)], axis=0)
        for part in split(lines):
            term = dot(sel[b], part, ((1,), (1,)))
            payload = term if payload is None else payload + term
    ts[:, 0:32, :] = payload[:, 0:256].reshape(NG, 32, 256)
    rest = payload[:, 256:384].reshape(NG, 4, 8, 128)
    left = lax.broadcasted_iota(jnp.int32, (NG, 8, 128), 2) < 64
    for e in range(2):
        moved = pltpu.roll(rest[:, 2 * e + 1].reshape(NG * 8, 128), 64, 1).reshape(NG, 8, 128)
        ts[:, 32:40, 128 * e : 128 * e + 128] = jnp.where(left, rest[:, 2 * e], moved)

    @pl.when(jnp.logical_not(is_outlet))
    def _():
        pl.semaphore_wait(barrier, NG + NK - 2)

    leaving = []
    coming = {}

    def batch(name, source, target, send, receive):
        whole = pltpu.make_async_remote_copy(
            source, target, send, receive, device_id={"gx": along_gx(1)}, device_id_type=MESH
        )
        leaving.append(whole.wait_send)
        coming[name] = whole.wait_recv

    def arrive(name):
        coming.pop(name)()

    for j in range(1, NG):
        pltpu.make_async_remote_copy(
            ts.at[along_gx(j)], tr.at[g], tile_ss.at[0], tile_rs.at[0],
            device_id={"gx": along_gx(j)}, device_id_type=MESH,
        ).start()
    batch("tiles", ts.at[1:NG], tr.at[1:NG], tile_ss.at[0], tile_rs.at[0])

    tr[g] = ts[g]

    @pl.when(is_inlet)
    def _():
        inflow_copy().wait_recv()
        for j in INLET_ORDER:
            pltpu.make_async_remote_copy(
                inlet.at[mine], inlet.at[mine], in_ss.at[1], in_rs.at[1],
                device_id={"yz": along_yz(j)}, device_id_type=MESH,
            ).start()

    loads[2].wait()

    def place_row(j, counts):
        counts = list(counts)
        for t in range(2):
            rows = []
            for e in range(2):
                goal = (receptors[2 * j + e] - 32 * t) * 8
                one = jnp.where(offset == goal, 1.0, 0.0)
                counts[t] = counts[t] + one
                rows.append(one)
            place[t, pl.ds(pl.multiple_of(16 * j, 16), 16), :] = jnp.concatenate(rows, axis=0).astype(BF16)
        return tuple(counts)

    counts = lax.fori_loop(0, SLOTS // 2, place_row, (jnp.zeros((8, CZ), F32),) * 2)

    loads[3].wait()

    def patch_copy(j):
        return pltpu.make_async_remote_copy(
            patch_s.at[j], patch_r, patch_ss.at[j], patch_rs.at[0], device_id={"gx": j}, device_id_type=MESH,
        )

    @pl.when(is_inlet)
    def _():
        inlet_rows[:, 32:48, :] = jnp.zeros((2, 16, CZ), F32)

        inlet_copies().wait_recv()

        for y in range(CY):
            row = inlet[pl.ds(inflow[y], 1), :]
            for f in range(5):
                cells = row[:, f * CZ : (f + 1) * CZ]
                at = (y % 8) * 5 + f
                u0[y, f, 0:1, :] = cells
                inlet_rows[y // 8, at : at + 1, :] = cells
        total = None
        for b in range(2):
            lines = jnp.concatenate([inlet_rows[b], jnp.zeros((80, CZ), F32)], axis=0)
            for part in split(lines):
                term = dot(sel[b], part, ((1,), (1,)))
                total = term if total is None else total + term
        patch_s[...] = total.reshape(NG, 32, 128)

        @pl.loop(1, NG)
        def _(j):
            patch_copy(j).start()

        patch_r[...] = patch_s[0]

    arrive("tiles")

    main = tr[:, 0:32, :].reshape(512, 256)
    rest = []
    for e in range(2):
        two = tr[:, 32:40, 128 * e : 128 * e + 128]
        rest += [two, pltpu.roll(two.reshape(NG * 8, 128), 64, 1).reshape(NG, 8, 128)]
    rest = jnp.stack(rest, axis=1).reshape(512, 128)
    halves_of = [split(main), split(rest)]
    for t in range(2):
        total = jnp.concatenate(
            [
                dot(high, place[t], ((0,), (0,))) + dot(low, place[t], ((0,), (0,)))
                for high, low in halves_of
            ],
            axis=0,
        )
        hits = jnp.sum(counts[t], axis=0, keepdims=True)
        scale = (1.0 / jnp.maximum(hits, 1.0)).reshape(1, 1, 1, CZ)
        mean = total[:320].reshape(8, 5, 8, CZ) * scale
        value = jnp.where(hits.reshape(1, 1, 1, CZ) > 0, mean, u0[8 * t : 8 * t + 8])
        for f in range(5):
            u[f, 8 * t : 8 * t + 8] = value[:, f]

    @pl.when(sect == 1)
    def _():
        @pl.when(g > 0)
        def _():
            patch_copy(g).wait_recv()

        column = lax.broadcasted_iota(jnp.int32, (128, 384), 1)
        spread = (column == 8 * lax.broadcasted_iota(jnp.int32, (128, 384), 0)).astype(F32).astype(BF16)
        wide = None
        for part in split(patch_r[...]):
            term = dot(part, spread)
            wide = term if wide is None else wide + term
        high, low = split(wide)
        for t in range(2):
            rows = place[t, 0:32, :]
            total = dot(high, rows, ((0,), (0,))) + dot(low, rows, ((0,), (0,)))
            hits = jnp.sum(counts[t], axis=0, keepdims=True)
            value = (total * (1.0 / jnp.maximum(hits, 1.0)))[:320].reshape(8, 5, 8, CZ)
            for f in range(5):
                u[f, 8 * t : 8 * t + 8] += value[:, f]

    def start_all(name, source, target, send, receive, lo, hi, at):
        for j in range(1, NG):
            pltpu.make_async_remote_copy(
                source.at[lo:hi, along_gx(j)], target.at[lo:hi, g], send.at[at], receive.at[at],
                device_id={"gx": along_gx(j)}, device_id_type=MESH,
            ).start()
        batch((name, at), source.at[lo:hi, 1:NG], target.at[lo:hi, 1:NG], send.at[at], receive.at[at])
        target[lo:hi, g] = source[lo:hi, g]

    start_all("u", u, pu, u_ss, u_rs, 0, 5, 0)

    loads[4].wait()
    loads[5].wait()

    def mix(d, f, h):
        return jac[f, d, h] * (-SEGMENT_STEP)

    @pl.loop(0, CY)
    def _(y):
        cells = [u[h, y] for h in range(5)]
        for f in range(5):
            value = mix(1, f, 0) * cells[0]
            for h in range(1, 5):
                value += mix(1, f, h) * cells[h]
            v[f, y] = value

    def halo(operator, i):
        name, source, edge, reach = operator["name"], operator["source"], operator["edge"], operator["reach"]
        send, receive = operator["halo"]
        lo, hi = GROUPS[i]
        pltpu.make_async_remote_copy(
            source.at[lo:hi, CY - reach : CY], edge.at[lo:hi, 0:reach], send.at[i], receive.at[i],
            device_id={"yz": along_yz(1)}, device_id_type=MESH,
        ).start()
        pltpu.make_async_remote_copy(
            source.at[lo:hi, 0:reach], edge.at[lo:hi, reach : 2 * reach], send.at[i], receive.at[i],
            device_id={"yz": from_yz(1)}, device_id_type=MESH,
        ).start()
        batch((name, "halo", i), source.at[lo:hi, 0 : 2 * reach], edge.at[lo:hi], send.at[i], receive.at[i])

    def hops(name, source, target, sems, i):
        send, receive = sems
        for j in range(1, NK):
            pltpu.make_async_remote_copy(
                source.at[i, along_yz(j)], target.at[i, k], send.at[i], receive.at[i],
                device_id={"yz": along_yz(j)}, device_id_type=MESH,
            ).start()
        batch((name, i), source.at[i, 1:NK], target.at[i, 1:NK], send.at[i], receive.at[i])
        target[i, k] = source[i, k]

    def first_half(operator, i):
        source, phi, places = operator["source"], operator["phi"], operator["places"]
        lo, hi = GROUPS[i]
        direct = operator["direct"] == i
        planes, everyone = operator["planes"], operator["everyone"]
        for f in range(lo, hi if direct else lo + 2):
            for half in range(2):
                tile = (f - lo) * 2 + half
                if f >= hi:
                    phi[i, tile] = jnp.zeros((8, 128), F32)
                    phi[i, 4 + tile] = jnp.zeros((8, 128), F32)
                    continue
                up = down = None
                for y in range(CY):
                    row = source[f, y, :, 128 * half : 128 * half + 128]
                    a = table[places["send_up"] + k * CY + y] * row
                    b = table[places["send_down"] + k * CY + y] * row
                    up, down = (a, b) if up is None else (up + a, down + b)
                if direct:
                    planes[0, f - lo, :, 128 * half : 128 * half + 128] = up
                    planes[1, f - lo, :, 128 * half : 128 * half + 128] = down
                else:
                    phi[i, tile] = up
                    phi[i, 4 + tile] = down

        if direct:
            send, receive = operator["first"]
            for j in range(1, NK):
                peer = along_yz(j)
                pltpu.make_async_remote_copy(
                    planes.at[lax.div(k - peer + NK, NK)], everyone.at[k], send.at[i], receive.at[i],
                    device_id={"yz": peer}, device_id_type=MESH,
                ).start()
            whole = everyone.at[1:NK]
            batch((operator["name"] + "2", i), whole, whole, send.at[i], receive.at[i])
            halo(operator, i)
            return

        hops(operator["name"] + "1", phi, operator["col"], operator["first"], i)
        halo(operator, i)

    def second_half(operator, i):
        if operator["direct"] == i:
            return
        col, gam, places = operator["col"], operator["gam"], operator["places"]
        arrive((operator["name"] + "1", i))
        upward = lax.div(k, 4)
        tiles = [col[i, s] for s in range(NK)]

        @pl.loop(0, NK)
        def _(d):
            base = places["take"] + upward * (NK * NK) + d * NK
            total = table[base] * tiles[0]
            for s in range(1, NK):
                total += table[base + s] * tiles[s]
            gam[i, d] = total

        hops(operator["name"] + "2", gam, operator["got"], operator["second"], i)

    def y_lines(operator, i, stencil, side, store):
        source, got, edge, reach, places = (
            operator["source"], operator["got"], operator["edge"], operator["reach"], operator["places"],
        )
        lo, hi = GROUPS[i]
        arrive((operator["name"], "halo", i))
        arrive((operator["name"] + "2", i))

        def entry(name, count, index=0):
            return table[places[name] + k * count + index]

        for f in range(lo, hi):
            for half in range(2):
                lanes = slice(128 * half, 128 * half + 128)
                tile = (f - lo) * 2 + half
                if operator["direct"] == i:
                    from_low = from_high = None
                    for j in range(1, NK):
                        block = along_yz(j)
                        plane = operator["everyone"][block, f - lo, :, lanes]
                        a = table[places["take"] + k * NK + block] * plane
                        b = table[places["take"] + NK * NK + k * NK + block] * plane
                        from_low, from_high = (a, b) if from_low is None else (from_low + a, from_high + b)
                else:
                    from_low = got[i, tile]
                    from_high = got[i, 4 + tile]
                rows = [edge[f, h, :, lanes] * entry("has_low", 1) for h in range(reach)]
                rows += [source[f, y, :, lanes] for y in range(CY)]
                rows += [edge[f, reach + h, :, lanes] * entry("has_high", 1) for h in range(reach)]
                for h in range(reach):
                    from_low += entry("near_low", reach, h) * rows[h] + entry("own_low", reach, h) * rows[reach + h]
                    from_high += (
                        entry("near_high", reach, h) * rows[reach + CY + h]
                        + entry("own_high", reach, h) * rows[CY + h]
                    )
                moves = {}
                for move, factor in stencil:
                    moves.setdefault(abs(move), {})[move] = factor
                values = []
                for y in range(CY):
                    at = reach + y
                    value = None
                    for move, factors in moves.items():
                        if move == 0:
                            term = np.float32(factors[0]) * rows[at]
                        elif factors[move] == factors[-move]:
                            term = np.float32(factors[move]) * (rows[at + move] + rows[at - move])
                        else:
                            term = np.float32(factors[move]) * (rows[at + move] - rows[at - move])
                        value = term if value is None else value + term
                    if y == 0:
                        value = value + from_low
                    if y == CY - 1:
                        value = value + from_high
                    if y > 0:
                        value = value - entry("lower", CY, y) * values[-1]
                    values.append(value)
                last = None
                for y in range(CY - 1, -1, -1):
                    value = values[y] if last is None else values[y] - np.float32(side) * last
                    last = value * entry("inverse", CY, y)
                    store(y, f, half, last)

    deriv = dict(
        name="d", source=v, phi=phi_d, col=col_d, gam=gam_d, got=got_d, edge=edge_d, reach=2, places=at_d,
        first=(d1_ss, d1_rs), second=(d2_ss, d2_rs), halo=(dh_ss, dh_rs),
        direct=DIRECT_DERIV, planes=planes_d, everyone=everyone_d,
    )
    smooth = dict(
        name="f", source=sb, phi=phi_f, col=col_f, gam=gam_f, got=got_f, edge=edge_f, reach=5, places=at_f,
        first=(f1_ss, f1_rs), second=(f2_ss, f2_rs), halo=(fh_ss, fh_rs),
        direct=DIRECT_FILTER, planes=planes_f, everyone=everyone_f,
    )

    def store_q(y, f, half, value):
        q[f, y, :, 128 * half : 128 * half + 128] = value

    def store_out(y, f, half, value):
        start = y * CZ + 128 * half
        out[0, f, :, start : start + 128] = value

    count = len(GROUPS)
    def q_lines(i):
        y_lines(deriv, i, DERIV_STENCIL, SIDE_DERIV, store_q)
        start_all("q", q, pq, q_ss, q_rs, *GROUPS[i], i)

    for i in range(count):
        first_half(deriv, i)
    for i in range(1, count):
        second_half(deriv, i)
    for i in range(count):
        q_lines(i)

    for load in loads[6:]:
        load.wait()
    arrive(("u", 0))
    for f in range(5):
        high, low = split(pu[f].reshape(NX, CZ))
        gx_[f] = dot(dx[sect, 0], high) + dot(dx[sect, 0], low) + dot(dx[sect, 1], high)
        gz_[f] = dot(high, dz[0]) + dot(low, dz[0]) + dot(high, dz[1])

    @pl.loop(0, 5)
    def _(f):
        value = pu[f].reshape(NX, CZ)
        for h in range(5):
            value += mix(0, f, h) * gx_[h]
            value += mix(2, f, h) * gz_[h]
        pp[f] = value

    for i in range(count):
        lo, hi = GROUPS[i]
        arrive(("q", i))
        for f in range(lo, hi):
            high, low = split(pp[f] + pq[f].reshape(NX, CZ))
            value = dot(high, fz[0]) + dot(low, fz[0]) + dot(high, fz[1])
            high, low = split(value)
            value = dot(fx[sect, 0], high) + dot(fx[sect, 0], low) + dot(fx[sect, 1], high)
            ps[f] = value.reshape(NG, CX, CZ)
        start_all("s", ps, sb, s_ss, s_rs, lo, hi, i)

    for i in range(count):
        arrive(("s", i))
        first_half(smooth, i)
        if i > 0:
            second_half(smooth, i - 1)
    for i in range(count):
        y_lines(smooth, i, FILTER_STENCIL, SIDE_FILTER, store_out)

    for wait in leaving:
        wait()

    @pl.when(is_outlet)
    def _():
        inflow_copy().wait_send()

    @pl.when(is_inlet)
    def _():
        inlet_copies().wait_send()

        @pl.loop(1, NG)
        def _(j):
            patch_copy(j).wait_send()


def per_device(fields, jacobians, inflow_map, donor_tiles, receptor_tiles):
    table_d, places_d = block_table(DERIV_STENCIL, SIDE_DERIV)
    table_f, places_f = block_table(FILTER_STENCIL, SIDE_FILTER)
    places_f = {name: start + table_d.size for name, start in places_f.items()}
    table = np.concatenate([table_d, table_f]).astype(np.float32)
    dx = np.stack([halves(line_matrix(NX, p, DERIV_STENCIL, SIDE_DERIV)) for p in (True, False)])
    fx = np.stack([halves(line_matrix(NX, p, FILTER_STENCIL, SIDE_FILTER)) for p in (True, False)])
    dz = halves(line_matrix(CZ, True, DERIV_STENCIL, SIDE_DERIV).T)
    fz = halves(line_matrix(CZ, True, FILTER_STENCIL, SIDE_FILTER).T)
    block = (5, CY, CX, CZ)
    count = len(GROUPS)

    def buffer(*shape, kind=F32):
        return pltpu.VMEM(shape, kind)

    def scalars(*shape, kind=jnp.int32):
        return pltpu.SMEM(shape, kind)

    def dma(length):
        return pltpu.SemaphoreType.DMA((length,))

    tiles = [buffer(count, NK, 8, 128)] * 4
    inputs = (
        fields, jnp.transpose(jacobians, (1, 0, 2)), inflow_map, jnp.transpose(donor_tiles, (0, 1, 4, 2, 3)),
        receptor_tiles.reshape(SLOTS), jnp.asarray(table), jnp.asarray(dx), jnp.asarray(fx), jnp.asarray(dz),
        jnp.asarray(fz),
    )
    return pl.pallas_call(
        functools.partial(kernel, places_d, places_f),
        out_shape=jax.ShapeDtypeStruct(fields.shape, F32),
        in_specs=[pl.BlockSpec(memory_space=HBM)] * len(inputs),
        out_specs=pl.BlockSpec(memory_space=pltpu.VMEM),
        scratch_shapes=[
            buffer(*fields.shape), scalars(5, 3, 5, kind=F32), scalars(16), scalars(1, 1, 3, 1, SLOTS), scalars(SLOTS),
            scalars(table.size, kind=F32),
            buffer(*dx.shape, kind=BF16), buffer(*fx.shape, kind=BF16),
            buffer(*dz.shape, kind=BF16), buffer(*fz.shape, kind=BF16), dma(10),
            buffer(CY, 5, CX, CZ),
            buffer(2, 512, CZ, kind=BF16), buffer(2, 512, CZ, kind=BF16),
            buffer(NG, 40, 256), buffer(NG, 40, 256),
            buffer(*block), buffer(*block), buffer(*block), buffer(*block), buffer(*block),
            buffer(5, NX, CZ), buffer(5, NX, CZ), buffer(5, NX, CZ),
            buffer(*block), buffer(*block),
            buffer(CY, 5 * CZ), buffer(NY, 5 * CZ), buffer(2, 48, CZ), buffer(NG, 32, 128), buffer(32, 128),
            *tiles, *tiles,
            buffer(5, 4, CX, CZ), buffer(5, 10, CX, CZ),
            buffer(2, 2, CX, CZ), buffer(NK, 2, CX, CZ), buffer(2, 1, CX, CZ), buffer(NK, 1, CX, CZ),
            *([dma(1)] * 4), *([dma(count)] * 16), dma(2), dma(2), dma(NG), dma(1),
        ],
        compiler_params=pltpu.CompilerParams(
            collective_id=0, has_side_effects=True, vmem_limit_bytes=VMEM_MIB * 1024 * 1024
        ),
        name="segment",
    )(*inputs)


def solution(mesh):
    in_specs = (
        P("sect", None, "gx", "yz"),
        P(),
        P("yz"),
        P("sect", "gx", "yz", None, None),
        P("sect", "gx", "yz", None),
    )
    out_specs = P("sect", None, "gx", "yz")
    return jax.shard_map(
        per_device, mesh=mesh, in_specs=in_specs, out_specs=out_specs, check_vma=False
    )
```

time: 101 us -> 67.5 us (0.67)
  the two profiles are of different devices: /device:TPU:28 before, /device:TPU:16 now
where the time goes in v1:
time: 67.5 us; the launch traced here: 67.4 us
  Pallas kernels  65.4 us (97%)
  local copies, waits for them, and re-layouts  1.97 us (3%)
    pallas_call x1, Pallas kernels, per_device(): pl.pallas_call(functools.partial(kernel, places_d, places_f), out_shape=j...  65.4 us
    unnamed x1, local copies, waits for them, and re-layouts  1.97 us

profile of v1, /device:TPU:16, one launch (start us, length us, event | category | flops | bytes accessed | tf_op | source)
XLA Modules:
  0.0 67.4 jit_solution(14790934086891469284)
XLA Ops:
  0.0 65.4 %segment.1 = f32[1,5,8,4096]{3,2,1,0:T(8,128)} custom-call(f32[1,5,8,4096]{3,2,1,0:T(8,128)} %fields_hbm.1, f32[5,3,5]{2,1,0:T(4,128)} %bitcast.3, s32[16]{0:T(128)} %inflow_hbm.1, s32[1,1,3,1,64]{4,3,2,1,0:T(1,128)} %bitcast.4, s32[64]{0:T(128)} %bitcast.5, f32[1536]{0:T(1024)} %constant.10.clone.table_hbm, bf16[2,2,128,128]{3,2,1,0:T(8,128)(2,1)} %constant.11.clone.dx_hbm, ...), custom_call_target="tpu_custom_call" | custom-call | tf_op jit(solution)/shard_map/segment/pallas_call | solution.py:678
  65.4 2.0 %copy.12 = f32[1,5,8,4096]{3,2,1,0:T(8,128)} copy(f32[1,5,8,4096]{3,2,1,0:T(8,128)} %segment.1) | data formatting | bytes 1310720

commit v2 on v1

--- a/solution.py
+++ b/solution.py
@@ -25,8 +25,8 @@
 GROUPS = ((0, 2), (2, 4), (4, 5))
 VMEM_MIB = 62
 INLET_ORDER = (4, 3, 5, 2, 6, 1, 7)
-DIRECT_DERIV = 0
-DIRECT_FILTER = 2
+DIRECT_DERIV = (0, 1, 2)
+DIRECT_FILTER = (2,)
 
 SEGMENT_STEP = 0.25
 SIDE_DERIV = 1.0 / 3.0
@@ -164,8 +164,10 @@
     u0, sel, place, ts, tr, u, pu, v, q, pq, gx_, gz_, pp, ps, sb,
     outlet, inlet, inlet_rows, patch_s, patch_r,
     phi_d, col_d, gam_d, got_d, phi_f, col_f, gam_f, got_f, edge_d, edge_f, planes_d, everyone_d, planes_f, everyone_f,
+    du, pdu, dv, planes_x, everyone_x, edge_x,
     tile_ss, tile_rs, u_ss, u_rs, q_ss, q_rs, s_ss, s_rs,
     d1_ss, d1_rs, d2_ss, d2_rs, f1_ss, f1_rs, f2_ss, f2_rs, dh_ss, dh_rs, fh_ss, fh_rs, in_ss, in_rs, patch_ss, patch_rs,
+    du_ss, du_rs, x_ss, x_rs,
 ):
     sect = lax.axis_index("sect")
     g = lax.axis_index("gx")
@@ -322,33 +324,6 @@
         return pltpu.make_async_remote_copy(
             patch_s.at[j], patch_r, patch_ss.at[j], patch_rs.at[0], device_id={"gx": j}, device_id_type=MESH,
         )
-
-    @pl.when(is_inlet)
-    def _():
-        inlet_rows[:, 32:48, :] = jnp.zeros((2, 16, CZ), F32)
-
-        inlet_copies().wait_recv()
-
-        for y in range(CY):
-            row = inlet[pl.ds(inflow[y], 1), :]
-            for f in range(5):
-                cells = row[:, f * CZ : (f + 1) * CZ]
-                at = (y % 8) * 5 + f
-                u0[y, f, 0:1, :] = cells
-                inlet_rows[y // 8, at : at + 1, :] = cells
-        total = None
-        for b in range(2):
-            lines = jnp.concatenate([inlet_rows[b], jnp.zeros((80, CZ), F32)], axis=0)
-            for part in split(lines):
-                term = dot(sel[b], part, ((1,), (1,)))
-                total = term if total is None else total + term
-        patch_s[...] = total.reshape(NG, 32, 128)
-
-        @pl.loop(1, NG)
-        def _(j):
-            patch_copy(j).start()
-
-        patch_r[...] = patch_s[0]
 
     arrive("tiles")
 
@@ -374,27 +349,6 @@
         for f in range(5):
             u[f, 8 * t : 8 * t + 8] = value[:, f]
 
-    @pl.when(sect == 1)
-    def _():
-        @pl.when(g > 0)
-        def _():
-            patch_copy(g).wait_recv()
-
-        column = lax.broadcasted_iota(jnp.int32, (128, 384), 1)
-        spread = (column == 8 * lax.broadcasted_iota(jnp.int32, (128, 384), 0)).astype(F32).astype(BF16)
-        wide = None
-        for part in split(patch_r[...]):
-            term = dot(part, spread)
-            wide = term if wide is None else wide + term
-        high, low = split(wide)
-        for t in range(2):
-            rows = place[t, 0:32, :]
-            total = dot(high, rows, ((0,), (0,))) + dot(low, rows, ((0,), (0,)))
-            hits = jnp.sum(counts[t], axis=0, keepdims=True)
-            value = (total * (1.0 / jnp.maximum(hits, 1.0)))[:320].reshape(8, 5, 8, CZ)
-            for f in range(5):
-                u[f, 8 * t : 8 * t + 8] += value[:, f]
-
     def start_all(name, source, target, send, receive, lo, hi, at):
         for j in range(1, NG):
             pltpu.make_async_remote_copy(
@@ -403,8 +357,6 @@
             ).start()
         batch((name, at), source.at[lo:hi, 1:NG], target.at[lo:hi, 1:NG], send.at[at], receive.at[at])
         target[lo:hi, g] = source[lo:hi, g]
-
-    start_all("u", u, pu, u_ss, u_rs, 0, 5, 0)
 
     loads[4].wait()
     loads[5].wait()
@@ -448,7 +400,7 @@
     def first_half(operator, i):
         source, phi, places = operator["source"], operator["phi"], operator["places"]
         lo, hi = GROUPS[i]
-        direct = operator["direct"] == i
+        direct = i in operator["direct"]
         planes, everyone = operator["planes"], operator["everyone"]
         for f in range(lo, hi if direct else lo + 2):
             for half in range(2):
@@ -464,8 +416,8 @@
                     b = table[places["send_down"] + k * CY + y] * row
                     up, down = (a, b) if up is None else (up + a, down + b)
                 if direct:
-                    planes[0, f - lo, :, 128 * half : 128 * half + 128] = up
-                    planes[1, f - lo, :, 128 * half : 128 * half + 128] = down
+                    planes[0, f, :, 128 * half : 128 * half + 128] = up
+                    planes[1, f, :, 128 * half : 128 * half + 128] = down
                 else:
                     phi[i, tile] = up
                     phi[i, 4 + tile] = down
@@ -475,10 +427,10 @@
             for j in range(1, NK):
                 peer = along_yz(j)
                 pltpu.make_async_remote_copy(
-                    planes.at[lax.div(k - peer + NK, NK)], everyone.at[k], send.at[i], receive.at[i],
+                    planes.at[lax.div(k - peer + NK, NK), lo:hi], everyone.at[k, lo:hi], send.at[i], receive.at[i],
                     device_id={"yz": peer}, device_id_type=MESH,
                 ).start()
-            whole = everyone.at[1:NK]
+            whole = everyone.at[1:NK, lo:hi]
             batch((operator["name"] + "2", i), whole, whole, send.at[i], receive.at[i])
             halo(operator, i)
             return
@@ -487,7 +439,7 @@
         halo(operator, i)
 
     def second_half(operator, i):
-        if operator["direct"] == i:
+        if i in operator["direct"]:
             return
         col, gam, places = operator["col"], operator["gam"], operator["places"]
         arrive((operator["name"] + "1", i))
@@ -509,8 +461,9 @@
             operator["source"], operator["got"], operator["edge"], operator["reach"], operator["places"],
         )
         lo, hi = GROUPS[i]
-        arrive((operator["name"], "halo", i))
-        arrive((operator["name"] + "2", i))
+        if operator["name"] == "f":
+            arrive(("f", "halo", i))
+            arrive(("f2", i))
 
         def entry(name, count, index=0):
             return table[places[name] + k * count + index]
@@ -519,11 +472,11 @@
             for half in range(2):
                 lanes = slice(128 * half, 128 * half + 128)
                 tile = (f - lo) * 2 + half
-                if operator["direct"] == i:
+                if i in operator["direct"]:
                     from_low = from_high = None
                     for j in range(1, NK):
                         block = along_yz(j)
-                        plane = operator["everyone"][block, f - lo, :, lanes]
+                        plane = operator["everyone"][block, f, :, lanes]
                         a = table[places["take"] + k * NK + block] * plane
                         b = table[places["take"] + NK * NK + k * NK + block] * plane
                         from_low, from_high = (a, b) if from_low is None else (from_low + a, from_high + b)
@@ -590,9 +543,139 @@
         y_lines(deriv, i, DERIV_STENCIL, SIDE_DERIV, store_q)
         start_all("q", q, pq, q_ss, q_rs, *GROUPS[i], i)
 
+    before = len(leaving)
     for i in range(count):
         first_half(deriv, i)
-    for i in range(1, count):
+    early = len(leaving)
+
+    @pl.when(is_inlet)
+    def _():
+        inlet_rows[...] = jnp.zeros((2, 64, CZ), F32)
+        inlet_copies().wait_recv()
+        for y in range(CY):
+            row = inlet[pl.ds(inflow[y], 1), :]
+            for f in range(5):
+                at = (y % 8) * 8 + f
+                inlet_rows[y // 8, at : at + 1, :] = row[:, f * CZ : (f + 1) * CZ]
+        total = None
+        for b in range(2):
+            lines = jnp.concatenate([inlet_rows[b], jnp.zeros((64, CZ), F32)], axis=0)
+            for part in split(lines):
+                term = dot(sel[b], part, ((1,), (1,)))
+                total = term if total is None else total + term
+        total = total.reshape(NG, 2, 16, 128)
+        moved = pltpu.roll(total[:, 1].reshape(NG * 16, 128), 64, 1).reshape(NG, 16, 128)
+        side = lax.broadcasted_iota(jnp.int32, (NG, 16, 128), 2) < 64
+        patch_s[...] = jnp.where(side, total[:, 0], moved)
+
+        @pl.loop(1, NG)
+        def _(j):
+            patch_copy(j).start()
+
+        patch_r[...] = patch_s[0]
+
+    start_all("u", u, pu, u_ss, u_rs, 0, 5, 0)
+    def plane_copy(j):
+        return pltpu.make_async_remote_copy(
+            du.at[along_gx(j)], pdu.at[g], du_ss.at[0], du_rs.at[0],
+            device_id={"gx": along_gx(j)}, device_id_type=MESH,
+        )
+
+    def plane_copies():
+        return pltpu.make_async_remote_copy(
+            du.at[1:NG], pdu.at[1:NG], du_ss.at[0], du_rs.at[0], device_id={"gx": along_gx(1)}, device_id_type=MESH,
+        )
+
+    @pl.when(sect == 1)
+    def _():
+        @pl.when(g > 0)
+        def _():
+            patch_copy(g).wait_recv()
+
+        packed = patch_r[...]
+        high, low = split(jnp.concatenate([packed, pltpu.roll(packed, 64, 1)], axis=0))
+        for t in range(2):
+            rows = place[t, 0:32, :]
+            total = dot(high, rows, ((0,), (0,))) + dot(low, rows, ((0,), (0,)))
+            hits = jnp.sum(counts[t], axis=0, keepdims=True)
+            value = (total[:64] * (1.0 / jnp.maximum(hits, 1.0))).reshape(8, 8, CZ)
+            du[8 * t : 8 * t + 8] = value
+
+            @pl.when(g == 0)
+            def _():
+                taken = hits.reshape(1, 1, CZ) > 0
+                du[8 * t : 8 * t + 8] = jnp.where(taken, value, inlet_rows[t].reshape(8, 8, CZ))
+
+        row_of = lax.broadcasted_iota(jnp.int32, (8, CZ), 0)
+        factors = []
+        for h in range(5):
+            factor = jnp.zeros((8, CZ), F32)
+            for f in range(5):
+                factor = jnp.where(row_of == f, mix(1, f, h), factor)
+            factors.append(factor)
+        for y in range(CY):
+            value = factors[0] * du[y, 0:1, :]
+            for h in range(1, 5):
+                value += factors[h] * du[y, h : h + 1, :]
+            dv[y] = value
+        up = down = None
+        for y in range(CY):
+            a = table[at_d["send_up"] + k * CY + y] * dv[y]
+            b = table[at_d["send_down"] + k * CY + y] * dv[y]
+            up, down = (a, b) if up is None else (up + a, down + b)
+        planes_x[0] = up
+        planes_x[1] = down
+        for j in range(1, NK):
+            peer = along_yz(j)
+            pltpu.make_async_remote_copy(
+                planes_x.at[lax.div(k - peer + NK, NK)], everyone_x.at[k], x_ss.at[0], x_rs.at[0],
+                device_id={"yz": peer}, device_id_type=MESH,
+            ).start()
+        pltpu.make_async_remote_copy(
+            dv.at[CY - 2 : CY], edge_x.at[0:2], x_ss.at[1], x_rs.at[1],
+            device_id={"yz": along_yz(1)}, device_id_type=MESH,
+        ).start()
+        pltpu.make_async_remote_copy(
+            dv.at[0:2], edge_x.at[2:4], x_ss.at[1], x_rs.at[1],
+            device_id={"yz": from_yz(1)}, device_id_type=MESH,
+        ).start()
+
+    def extra_copies():
+        return [
+            pltpu.make_async_remote_copy(
+                whole, whole, x_ss.at[i], x_rs.at[i], device_id={"yz": along_yz(1)}, device_id_type=MESH,
+            )
+            for i, whole in enumerate((everyone_x.at[1:NK], edge_x))
+        ]
+
+    for wait in leaving[before:early]:
+        wait()
+    del leaving[before:early]
+
+    for i in range(count):
+        arrive(("d", "halo", i))
+        arrive(("d2", i))
+
+    @pl.when(sect == 1)
+    def _():
+        @pl.loop(1, NG)
+        def _(j):
+            plane_copy(j).start()
+
+        pdu[g] = du[g]
+        for y in range(CY):
+            for f in range(5):
+                v[f, y, 0:1, :] = v[f, y, 0:1, :] + dv[y, f : f + 1, :]
+        for copy in extra_copies():
+            copy.wait_recv()
+        for f in range(5):
+            for h in range(4):
+                edge_d[f, h, 0:1, :] = edge_d[f, h, 0:1, :] + edge_x[h, f : f + 1, :]
+            for j in range(1, NK):
+                block = along_yz(j)
+                everyone_d[block, f, 0:1, :] = everyone_d[block, f, 0:1, :] + everyone_x[block, f : f + 1, :]
+
+    for i in range(count):
         second_half(deriv, i)
     for i in range(count):
         q_lines(i)
@@ -600,6 +683,16 @@
     for load in loads[6:]:
         load.wait()
     arrive(("u", 0))
+
+    @pl.when(sect == 1)
+    def _():
+        plane_copies().wait_recv()
+
+        @pl.loop(0, NG)
+        def _(r):
+            for f in range(5):
+                pu[f, r, 0:1, :] = pu[f, r, 0:1, :] + pdu[r, f : f + 1, :]
+
     for f in range(5):
         high, low = split(pu[f].reshape(NX, CZ))
         gx_[f] = dot(dx[sect, 0], high) + dot(dx[sect, 0], low) + dot(dx[sect, 1], high)
@@ -634,6 +727,12 @@
 
     for wait in leaving:
         wait()
+
+    @pl.when(sect == 1)
+    def _():
+        plane_copies().wait_send()
+        for copy in extra_copies():
+            copy.wait_send()
 
     @pl.when(is_outlet)
     def _():
@@ -691,11 +790,12 @@
             buffer(*block), buffer(*block), buffer(*block), buffer(*block), buffer(*block),
             buffer(5, NX, CZ), buffer(5, NX, CZ), buffer(5, NX, CZ),
             buffer(*block), buffer(*block),
-            buffer(CY, 5 * CZ), buffer(NY, 5 * CZ), buffer(2, 48, CZ), buffer(NG, 32, 128), buffer(32, 128),
+            buffer(CY, 5 * CZ), buffer(NY, 5 * CZ), buffer(2, 64, CZ), buffer(NG, 16, 128), buffer(16, 128),
             *tiles, *tiles,
             buffer(5, 4, CX, CZ), buffer(5, 10, CX, CZ),
-            buffer(2, 2, CX, CZ), buffer(NK, 2, CX, CZ), buffer(2, 1, CX, CZ), buffer(NK, 1, CX, CZ),
-            *([dma(1)] * 4), *([dma(count)] * 16), dma(2), dma(2), dma(NG), dma(1),
+            *([buffer(2, 5, CX, CZ), buffer(NK, 5, CX, CZ)] * 2),
+            buffer(CY, 8, CZ), buffer(NG, 8, CZ), buffer(CY, 8, CZ), buffer(2, 8, CZ), buffer(NK, 8, CZ), buffer(4, 8, CZ),
+            *([dma(1)] * 4), *([dma(count)] * 16), dma(2), dma(2), dma(NG), dma(1), dma(1), dma(1), dma(2), dma(2),
         ],
         compiler_params=pltpu.CompilerParams(
             collective_id=0, has_side_effects=True, vmem_limit_bytes=VMEM_MIB * 1024 * 1024

time: 67.5 us -> 62.8 us (0.930)
  Pallas kernels: 65.4 us -> 60.4 us
    pallas_call x1, Pallas kernels: 65.4 us -> 60.4 us  [per_device(): pl.pallas_call(functools.partial(kernel, places_d, places_f), out_shape=j...]
where the time goes in v2:
time: 62.8 us; the launch traced here: 62.3 us
  Pallas kernels  60.4 us (96%)
  local copies, waits for them, and re-layouts  1.97 us (3%)
    pallas_call x1, Pallas kernels, per_device(): pl.pallas_call(functools.partial(kernel, places_d, places_f), out_shape=j...  60.4 us
    unnamed x1, local copies, waits for them, and re-layouts  1.97 us

profile of v2, /device:TPU:16, one launch (start us, length us, event | category | flops | bytes accessed | tf_op | source)
XLA Modules:
  0.0 62.3 jit_solution(5238046394065219213)
XLA Ops:
  0.0 60.4 %segment.1 = f32[1,5,8,4096]{3,2,1,0:T(8,128)} custom-call(f32[1,5,8,4096]{3,2,1,0:T(8,128)} %fields_hbm.1, f32[5,3,5]{2,1,0:T(4,128)} %bitcast.3, s32[16]{0:T(128)} %inflow_hbm.1, s32[1,1,3,1,64]{4,3,2,1,0:T(1,128)} %bitcast.4, s32[64]{0:T(128)} %bitcast.5, f32[1536]{0:T(1024)} %constant.10.clone.table_hbm, bf16[2,2,128,128]{3,2,1,0:T(8,128)(2,1)} %constant.11.clone.dx_hbm, ...), custom_call_target="tpu_custom_call" | custom-call | tf_op jit(solution)/shard_map/segment/pallas_call | solution.py:777
  60.4 2.0 %copy.12 = f32[1,5,8,4096]{3,2,1,0:T(8,128)} copy(f32[1,5,8,4096]{3,2,1,0:T(8,128)} %segment.1) | data formatting | bytes 1310720

commit v3 on v2

--- a/solution.py
+++ b/solution.py
@@ -24,8 +24,8 @@
 SLOTS = 64
 GROUPS = ((0, 2), (2, 4), (4, 5))
 VMEM_MIB = 62
+GX_ORDER = (8, 4, 12, 6, 10, 2, 14, 7, 9, 5, 11, 3, 13, 1, 15)
 INLET_ORDER = (4, 3, 5, 2, 6, 1, 7)
-DIRECT_DERIV = (0, 1, 2)
 DIRECT_FILTER = (2,)
 
 SEGMENT_STEP = 0.25
@@ -163,7 +163,7 @@
     fields, jac, inflow, donors, receptors, table, dx, fx, dz, fz, load_sem,
     u0, sel, place, ts, tr, u, pu, v, q, pq, gx_, gz_, pp, ps, sb,
     outlet, inlet, inlet_rows, patch_s, patch_r,
-    phi_d, col_d, gam_d, got_d, phi_f, col_f, gam_f, got_f, edge_d, edge_f, planes_d, everyone_d, planes_f, everyone_f,
+    phi_d, col_d, gam_d, got_d, phi_f, col_f, gam_f, got_f, edge_d, edge_f, planes_f, everyone_f,
     du, pdu, dv, planes_x, everyone_x, edge_x,
     tile_ss, tile_rs, u_ss, u_rs, q_ss, q_rs, s_ss, s_rs,
     d1_ss, d1_rs, d2_ss, d2_rs, f1_ss, f1_rs, f2_ss, f2_rs, dh_ss, dh_rs, fh_ss, fh_rs, in_ss, in_rs, patch_ss, patch_rs,
@@ -284,7 +284,7 @@
     def arrive(name):
         coming.pop(name)()
 
-    for j in range(1, NG):
+    for j in GX_ORDER:
         pltpu.make_async_remote_copy(
             ts.at[along_gx(j)], tr.at[g], tile_ss.at[0], tile_rs.at[0],
             device_id={"gx": along_gx(j)}, device_id_type=MESH,
@@ -350,7 +350,7 @@
             u[f, 8 * t : 8 * t + 8] = value[:, f]
 
     def start_all(name, source, target, send, receive, lo, hi, at):
-        for j in range(1, NG):
+        for j in GX_ORDER:
             pltpu.make_async_remote_copy(
                 source.at[lo:hi, along_gx(j)], target.at[lo:hi, g], send.at[at], receive.at[at],
                 device_id={"gx": along_gx(j)}, device_id_type=MESH,
@@ -523,7 +523,7 @@
     deriv = dict(
         name="d", source=v, phi=phi_d, col=col_d, gam=gam_d, got=got_d, edge=edge_d, reach=2, places=at_d,
         first=(d1_ss, d1_rs), second=(d2_ss, d2_rs), halo=(dh_ss, dh_rs),
-        direct=DIRECT_DERIV, planes=planes_d, everyone=everyone_d,
+        direct=(), planes=None, everyone=None,
     )
     smooth = dict(
         name="f", source=sb, phi=phi_f, col=col_f, gam=gam_f, got=got_f, edge=edge_f, reach=5, places=at_f,
@@ -542,6 +542,20 @@
     def q_lines(i):
         y_lines(deriv, i, DERIV_STENCIL, SIDE_DERIV, store_q)
         start_all("q", q, pq, q_ss, q_rs, *GROUPS[i], i)
+
+    def send_u():
+        for j in GX_ORDER:
+            pltpu.make_async_remote_copy(
+                u.at[:, along_gx(j)], pu.at[:, g], u_ss.at[0], u_rs.at[0],
+                device_id={"gx": along_gx(j)}, device_id_type=MESH,
+            ).start()
+
+    batch(("u", 0), u.at[:, 1:NG], pu.at[:, 1:NG], u_ss.at[0], u_rs.at[0])
+    pu[:, g] = u[:, g]
+
+    @pl.when(jnp.logical_not(is_inlet))
+    def _():
+        send_u()
 
     before = len(leaving)
     for i in range(count):
@@ -574,7 +588,12 @@
 
         patch_r[...] = patch_s[0]
 
-    start_all("u", u, pu, u_ss, u_rs, 0, 5, 0)
+    @pl.when(is_inlet)
+    def _():
+        send_u()
+
+    for i in range(count):
+        second_half(deriv, i)
     def plane_copy(j):
         return pltpu.make_async_remote_copy(
             du.at[along_gx(j)], pdu.at[g], du_ss.at[0], du_rs.at[0],
@@ -671,12 +690,21 @@
         for f in range(5):
             for h in range(4):
                 edge_d[f, h, 0:1, :] = edge_d[f, h, 0:1, :] + edge_x[h, f : f + 1, :]
-            for j in range(1, NK):
-                block = along_yz(j)
-                everyone_d[block, f, 0:1, :] = everyone_d[block, f, 0:1, :] + everyone_x[block, f : f + 1, :]
-
-    for i in range(count):
-        second_half(deriv, i)
+        from_low = from_high = None
+        for j in range(1, NK):
+            block = along_yz(j)
+            plane = everyone_x[block]
+            a = table[at_d["take"] + k * NK + block] * plane
+            b = table[at_d["take"] + NK * NK + k * NK + block] * plane
+            from_low, from_high = (a, b) if from_low is None else (from_low + a, from_high + b)
+        for i, (lo, hi) in enumerate(GROUPS):
+            for f in range(lo, hi):
+                for half in range(2):
+                    tile = (f - lo) * 2 + half
+                    lanes = slice(128 * half, 128 * half + 128)
+                    got_d[i, tile, 0:1, :] = got_d[i, tile, 0:1, :] + from_low[f : f + 1, lanes]
+                    got_d[i, 4 + tile, 0:1, :] = got_d[i, 4 + tile, 0:1, :] + from_high[f : f + 1, lanes]
+
     for i in range(count):
         q_lines(i)
 
@@ -793,7 +821,7 @@
             buffer(CY, 5 * CZ), buffer(NY, 5 * CZ), buffer(2, 64, CZ), buffer(NG, 16, 128), buffer(16, 128),
             *tiles, *tiles,
             buffer(5, 4, CX, CZ), buffer(5, 10, CX, CZ),
-            *([buffer(2, 5, CX, CZ), buffer(NK, 5, CX, CZ)] * 2),
+            buffer(2, 5, CX, CZ), buffer(NK, 5, CX, CZ),
             buffer(CY, 8, CZ), buffer(NG, 8, CZ), buffer(CY, 8, CZ), buffer(2, 8, CZ), buffer(NK, 8, CZ), buffer(4, 8, CZ),
             *([dma(1)] * 4), *([dma(count)] * 16), dma(2), dma(2), dma(NG), dma(1), dma(1), dma(1), dma(2), dma(2),
         ],

time: 62.8 us -> 62.2 us (level)
  no operation moved by 1% of the time
where the time goes in v3:
time: 62.2 us; the launch traced here: 62 us
  Pallas kernels  60 us (96%)
  local copies, waits for them, and re-layouts  1.97 us (3%)
    pallas_call x1, Pallas kernels, per_device(): pl.pallas_call(functools.partial(kernel, places_d, places_f), out_shape=j...  60 us
    unnamed x1, local copies, waits for them, and re-layouts  1.97 us

profile of v3, /device:TPU:16, one launch (start us, length us, event | category | flops | bytes accessed | tf_op | source)
XLA Modules:
  0.0 62.0 jit_solution(11516761769348194738)
XLA Ops:
  0.0 60.0 %segment.1 = f32[1,5,8,4096]{3,2,1,0:T(8,128)} custom-call(f32[1,5,8,4096]{3,2,1,0:T(8,128)} %fields_hbm.1, f32[5,3,5]{2,1,0:T(4,128)} %bitcast.3, s32[16]{0:T(128)} %inflow_hbm.1, s32[1,1,3,1,64]{4,3,2,1,0:T(1,128)} %bitcast.4, s32[64]{0:T(128)} %bitcast.5, f32[1536]{0:T(1024)} %constant.10.clone.table_hbm, bf16[2,2,128,128]{3,2,1,0:T(8,128)(2,1)} %constant.11.clone.dx_hbm, ...), custom_call_target="tpu_custom_call" | custom-call | tf_op jit(solution)/shard_map/segment/pallas_call | solution.py:805
  60.0 2.0 %copy.12 = f32[1,5,8,4096]{3,2,1,0:T(8,128)} copy(f32[1,5,8,4096]{3,2,1,0:T(8,128)} %segment.1) | data formatting | bytes 1310720

commit v4 on v3

--- a/solution.py
+++ b/solution.py
@@ -25,8 +25,8 @@
 GROUPS = ((0, 2), (2, 4), (4, 5))
 VMEM_MIB = 62
 GX_ORDER = (8, 4, 12, 6, 10, 2, 14, 7, 9, 5, 11, 3, 13, 1, 15)
-INLET_ORDER = (4, 3, 5, 2, 6, 1, 7)
-DIRECT_FILTER = (2,)
+INLET_ORDER = (4, 5, 3, 6, 2, 7, 1)
+DIRECT_FILTER = (1, 2)
 
 SEGMENT_STEP = 0.25
 SIDE_DERIV = 1.0 / 3.0

time: 62.2 us -> 62.7 us (level)
  no operation moved by 1% of the time
where the time goes in v4:
time: 62.7 us; the launch traced here: 62.5 us
  Pallas kernels  60.5 us (96%)
  local copies, waits for them, and re-layouts  1.97 us (3%)
    pallas_call x1, Pallas kernels, per_device(): pl.pallas_call(functools.partial(kernel, places_d, places_f), out_shape=j...  60.5 us
    unnamed x1, local copies, waits for them, and re-layouts  1.97 us

profile of v4, /device:TPU:16, one launch (start us, length us, event | category | flops | bytes accessed | tf_op | source)
XLA Modules:
  0.0 62.5 jit_solution(12780365958059385027)
XLA Ops:
  0.0 60.5 %segment.1 = f32[1,5,8,4096]{3,2,1,0:T(8,128)} custom-call(f32[1,5,8,4096]{3,2,1,0:T(8,128)} %fields_hbm.1, f32[5,3,5]{2,1,0:T(4,128)} %bitcast.3, s32[16]{0:T(128)} %inflow_hbm.1, s32[1,1,3,1,64]{4,3,2,1,0:T(1,128)} %bitcast.4, s32[64]{0:T(128)} %bitcast.5, f32[1536]{0:T(1024)} %constant.10.clone.table_hbm, bf16[2,2,128,128]{3,2,1,0:T(8,128)(2,1)} %constant.11.clone.dx_hbm, ...), custom_call_target="tpu_custom_call" | custom-call | tf_op jit(solution)/shard_map/segment/pallas_call | solution.py:805
  60.5 2.0 %copy.12 = f32[1,5,8,4096]{3,2,1,0:T(8,128)} copy(f32[1,5,8,4096]{3,2,1,0:T(8,128)} %segment.1) | data formatting | bytes 1310720

commit v5 on v3

--- a/solution.py
+++ b/solution.py
@@ -167,7 +167,7 @@
     du, pdu, dv, planes_x, everyone_x, edge_x,
     tile_ss, tile_rs, u_ss, u_rs, q_ss, q_rs, s_ss, s_rs,
     d1_ss, d1_rs, d2_ss, d2_rs, f1_ss, f1_rs, f2_ss, f2_rs, dh_ss, dh_rs, fh_ss, fh_rs, in_ss, in_rs, patch_ss, patch_rs,
-    du_ss, du_rs, x_ss, x_rs,
+    du_ss, du_rs, x_ss, x_rs, result, out_ss,
 ):
     sect = lax.axis_index("sect")
     g = lax.axis_index("gx")
@@ -536,7 +536,7 @@
 
     def store_out(y, f, half, value):
         start = y * CZ + 128 * half
-        out[0, f, :, start : start + 128] = value
+        result[0, f, :, start : start + 128] = value
 
     count = len(GROUPS)
     def q_lines(i):
@@ -752,6 +752,10 @@
             second_half(smooth, i - 1)
     for i in range(count):
         y_lines(smooth, i, FILTER_STENCIL, SIDE_FILTER, store_out)
+        lo, hi = GROUPS[i]
+        write = pltpu.make_async_copy(result.at[:, lo:hi], out.at[:, lo:hi], out_ss.at[i])
+        write.start()
+        leaving.append(write.wait)
 
     for wait in leaving:
         wait()
@@ -806,7 +810,7 @@
         functools.partial(kernel, places_d, places_f),
         out_shape=jax.ShapeDtypeStruct(fields.shape, F32),
         in_specs=[pl.BlockSpec(memory_space=HBM)] * len(inputs),
-        out_specs=pl.BlockSpec(memory_space=pltpu.VMEM),
+        out_specs=pl.BlockSpec(memory_space=HBM),
         scratch_shapes=[
             buffer(*fields.shape), scalars(5, 3, 5, kind=F32), scalars(16), scalars(1, 1, 3, 1, SLOTS), scalars(SLOTS),
             scalars(table.size, kind=F32),
@@ -823,7 +827,7 @@
             buffer(5, 4, CX, CZ), buffer(5, 10, CX, CZ),
             buffer(2, 5, CX, CZ), buffer(NK, 5, CX, CZ),
             buffer(CY, 8, CZ), buffer(NG, 8, CZ), buffer(CY, 8, CZ), buffer(2, 8, CZ), buffer(NK, 8, CZ), buffer(4, 8, CZ),
-            *([dma(1)] * 4), *([dma(count)] * 16), dma(2), dma(2), dma(NG), dma(1), dma(1), dma(1), dma(2), dma(2),
+            *([dma(1)] * 4), *([dma(count)] * 16), dma(2), dma(2), dma(NG), dma(1), dma(1), dma(1), dma(2), dma(2), buffer(*fields.shape), dma(count),
         ],
         compiler_params=pltpu.CompilerParams(
             collective_id=0, has_side_effects=True, vmem_limit_bytes=VMEM_MIB * 1024 * 1024

time: 62.2 us -> 62 us (level)
  no operation moved by 1% of the time
where the time goes in v5:
time: 62 us; the launch traced here: 61.9 us
  Pallas kernels  59.9 us (97%)
  local copies, waits for them, and re-layouts  1.97 us (3%)
    pallas_call x1, Pallas kernels, per_device(): pl.pallas_call(functools.partial(kernel, places_d, places_f), out_shape=j...  59.9 us
    unnamed x1, local copies, waits for them, and re-layouts  1.97 us

profile of v5, /device:TPU:16, one launch (start us, length us, event | category | flops | bytes accessed | tf_op | source)
XLA Modules:
  0.0 61.9 jit_solution(8634098762558922643)
XLA Ops:
  0.0 59.9 %segment.1 = f32[1,5,8,4096]{3,2,1,0:T(8,128)} custom-call(f32[1,5,8,4096]{3,2,1,0:T(8,128)} %fields_hbm.1, f32[5,3,5]{2,1,0:T(4,128)} %bitcast.3, s32[16]{0:T(128)} %inflow_hbm.1, s32[1,1,3,1,64]{4,3,2,1,0:T(1,128)} %bitcast.4, s32[64]{0:T(128)} %bitcast.5, f32[1536]{0:T(1024)} %constant.10.clone.table_hbm, bf16[2,2,128,128]{3,2,1,0:T(8,128)(2,1)} %constant.11.clone.dx_hbm, ...), custom_call_target="tpu_custom_call" | custom-call | tf_op jit(solution)/shard_map/segment/pallas_call | solution.py:809
  59.9 2.0 %copy.12 = f32[1,5,8,4096]{3,2,1,0:T(8,128)} copy(f32[1,5,8,4096]{3,2,1,0:T(8,128)} %segment.1) | data formatting | bytes 1310720
